TPU v7x, 32 devices: a whole 2x2x4 slice. The times are simulated.
32 devices in a mesh: groups: 2 (over y), expert: 4 (over z), cuts: 4 (over x, core).
Axes of the slice: x: 2, y: 2, z: 4, core: 2. Of those that a mesh axis runs over, the one named last changes fastest.
Arguments:
- tokens: bfloat16 [256, 4096], P(('groups', 'expert', 'cuts')), parts along dimension 0, may hold values from -30 to 30
- router_weight: bfloat16 [4096, 4], replicated, may hold values from -0.09375 to 0.09375
- gate_weight: bfloat16 [4, 4096, 8192], P('expert', None, 'cuts'), may hold values from -0.09375 to 0.09375
- up_weight: bfloat16 [4, 4096, 8192], P('expert', None, 'cuts'), may hold values from -0.09375 to 0.09375
- down_weight: bfloat16 [4, 8192, 4096], P('expert', 'cuts'), may hold values from -0.0625 to 0.0625
- expert_ids: int32 [256, 2], P(('groups', 'expert', 'cuts')), parts along dimension 0, may hold values from 0 to 3, all different within a row; in each aligned block of 8 rows (0 to 7, 8 to 15, ...) at most 4 rows name the same one
Outputs:
- mixed: bfloat16 [256, 4096], P(('groups', 'expert', 'cuts')), parts along dimension 0
- router_stats: float32 [4], P('groups'), parts along dimension 0
There are 2 independent parts, one for each index of `groups`. A program takes and returns all parts, laid end to end along the dimension named above; an argument that names none is the same for every part. Nothing has to cross between parts.
Inputs may be any that keep to these rules, and one draw needn't show every extreme that they name: `expert_ids`: each row names 2 different experts; among the 8 rows of one device (aligned blocks of rows) no expert is named by more than 4 rows, and in some blocks one expert is named by exactly 4 rows.
All inputs are finite; a program needn't handle non-finite values.
Results may differ from a plain program's by a relative error of at most 0.0058.
Values may be sent and summed in bfloat16 or wider, within the bound.
A program may use at most 128 MiB of HBM per device.

v0:
```python
import jax
import jax.numpy as jnp
from jax import lax
from jax.sharding import PartitionSpec as P


def shards(tokens, router_weight, gate_weight, up_weight, down_weight, expert_ids):
    rows_dev, width = tokens.shape
    experts = router_weight.shape[1]
    cuts = lax.axis_size("cuts")
    columns = lax.axis_size("expert")
    total_rows = rows_dev * cuts * columns
    capacity = rows_dev // 2
    logits = jnp.dot(tokens, router_weight, preferred_element_type=jnp.float32)
    exps = jnp.exp(logits)
    total = jnp.sum(exps, axis=1, keepdims=True)
    probs = exps / total
    log_total = jnp.log(total[:, 0])
    labels = jnp.arange(experts, dtype=jnp.int32)
    picks = (expert_ids[:, :, None] == labels[None, None, :]).astype(jnp.int32)
    member = jnp.sum(picks, axis=1)
    square_part = jnp.sum(log_total * log_total)
    prob_part = jnp.sum(probs, axis=0)
    count_part = jnp.sum(member, axis=0).astype(jnp.float32)
    square_sum, prob_sum, count_sum = lax.psum(
        (square_part, prob_part, count_part), ("expert", "cuts")
    )
    balance = experts * jnp.sum(prob_sum / total_rows * (count_sum / (total_rows * 2)))
    router_stats = jnp.stack([square_sum / total_rows, balance])
    chosen = jnp.sum(picks.astype(jnp.float32) * probs[:, None, :], axis=2)
    combine = chosen / jnp.sum(chosen, axis=1, keepdims=True)
    position = jnp.cumsum(member, axis=0) - member
    slot_labels = jnp.arange(capacity, dtype=jnp.int32)
    select = (member[:, :, None] > 0) & (position[:, :, None] == slot_labels[None, None, :])
    w_gate = gate_weight[0]
    w_up = up_weight[0]
    w_down = down_weight[0]
    outbox = jnp.einsum(
        "rej,rd->ejd", select.astype(jnp.bfloat16), tokens, preferred_element_type=jnp.float32
    ).astype(jnp.bfloat16)
    inbox = lax.all_to_all(outbox, "expert", split_axis=0, concat_axis=0, tiled=True)
    block = lax.all_gather(inbox, "cuts", axis=0, tiled=True)
    flat = block.reshape(-1, width)
    gate = jnp.dot(flat, w_gate, preferred_element_type=jnp.float32)
    upper = jnp.dot(flat, w_up, preferred_element_type=jnp.float32)
    hidden_flat = (jax.nn.silu(gate) * upper).astype(jnp.bfloat16)
    hidden = hidden_flat.reshape(block.shape[:-1] + (hidden_flat.shape[-1],))
    flat_hidden = hidden.reshape(-1, hidden.shape[-1])
    summed = lax.psum_scatter(
        jnp.dot(flat_hidden, w_down, preferred_element_type=jnp.float32),
        "cuts",
        scatter_dimension=0,
        tiled=True,
    )
    answer = summed.astype(jnp.bfloat16).reshape(experts, capacity, width)
    returned = lax.all_to_all(answer, "expert", split_axis=0, concat_axis=0, tiled=True)
    combine_expert = jnp.sum(picks.astype(jnp.float32) * combine[:, :, None], axis=1)
    weight_table = select.astype(jnp.float32) * combine_expert[:, :, None]
    mixed = jnp.einsum(
        "rej,ejd->rd", weight_table, returned.astype(jnp.float32), precision=lax.Precision.HIGHEST
    )
    return (mixed.astype(jnp.bfloat16), router_stats)


def solution(mesh):
    placed = (
        P(("groups", "expert", "cuts"), None),
        P(),
        P("expert", None, "cuts"),
        P("expert", None, "cuts"),
        P("expert", "cuts", None),
        P(("groups", "expert", "cuts"), None),
    )
    return jax.shard_map(
        shards,
        mesh=mesh,
        in_specs=placed,
        out_specs=(P(("groups", "expert", "cuts"), None), P("groups")),
        check_vma=False,
    )
```

profile of v0, /device:TPU:0, one launch (start us, length us, event | category | flops | bytes accessed | tf_op | source)
XLA Modules:
  0.0 104.9 jit_solution(15953216799917773635)
XLA Ops:
  7.2 0.0 copy-start
  7.2 0.0 reduce-scatter.2.cloned.1.call-start
  7.2 0.8 convert_reduce_fusion
  8.0 0.2 reduce_window_sum.11
  8.2 0.2 convolution_convert_fusion
  8.4 12.2 %all_to_all.10 = bf16[4,4,4096]{2,1,0:T(4,128)(2,1)S(1)} all-to-all(bf16[4,4,4096]{2,1,0:T(4,128)(2,1)S(1)} %convolution_convert_fusion), channel_id=1, replica_groups=mesh['groups'=2,'expert'=4,'cuts'=4] {'expert'}, dimensions={0} | all-to-all | bytes 262144 | tf_op jit(solution)/shard_map/all_to_all | solution.py:41
  20.6 7.2 %all_gather.3 = bf16[16,4,4096]{2,1,0:T(4,128)(2,1)S(1)} all-gather(bf16[4,4,4096]{2,1,0:T(4,128)(2,1)S(1)} %all_to_all.10), channel_id=1, replica_groups=mesh['groups'=2,'expert'=4,'cuts'=4] {'cuts'}, dimensions={0}, use_global_device_ids=true | all-gather | bytes 655360 | tf_op jit(solution)/shard_map/all_gather | solution.py:42
  27.8 0.1 reshape.45
  27.9 8.8 %fusion.4 = f32[64,2048]{1,0:T(8,128)S(1)} fusion(bf16[64,4096]{1,0:T(8,128)(2,1)S(1)} %reshape.45, bf16[1,4096,2048]{2,1,0:T(8,128)(2,1)} %param.8), kind=kOutput, calls=%fused_computation.4 | convolution fusion | flops 1073741824 | bytes 17825792 | tf_op jit(solution)/shard_map/dot_general | solution.py:44
  36.7 0.0 copy-start.2
  36.7 14.6 %fusion = f32[64,4096]{1,0:T(8,128)} fusion(bf16[1,2048,4096]{2,1,0:T(8,128)(2,1)} %param.10, bf16[64,4096]{1,0:T(8,128)(2,1)S(1)} %reshape.45, bf16[1,4096,2048]{2,1,0:T(8,128)(2,1)} %param.9, f32[64,2048]{1,0:T(8,128)S(1)} %fusion.4), kind=kOutput, calls=%fused_computation | convolution fusion | flops 2148270080 | bytes 35651584 | tf_op jit(solution)/shard_map/dot_general | solution.py:50
  51.3 0.0 reduce-scatter.2.cloned.1.call-update
  51.3 0.2 fusion.40
  51.5 0.6 multiply_reduce_fusion.1
  52.1 0.1 fusion.39
  52.3 32.0 %all-reduce = (f32[4]{0:T(128)S(1)}, f32[4]{0:T(128)S(1)}, f32[]{:T(128)}) all-reduce(f32[4]{0:T(128)S(1)} %convert_element_type.31, f32[4]{0:T(128)S(1)} %get-tuple-element.9, f32[]{:T(128)} %multiply_reduce_fusion.1), channel_id=1, replica_groups=mesh['groups'=2,'expert'=4,'cuts'=4] {'expert','cuts'}, use_global_device_ids=true, to_apply=%region_12.13 | all-reduce | flops 9 | bytes 72 | tf_op jit(solution)/shard_map/psum | solution.py:25
  84.2 0.6 multiply_reduce_fusion
  86.2 0.0 reduce-scatter.2.cloned.1.call-done
  86.2 1.0 convert_element_type.29
  87.2 0.7 reshape.46
  87.9 3.3 %all-to-all-start.1 = ((bf16[4,4,4096]{2,1,0:T(4,128)(2,1)}), bf16[4,4,4096]{2,1,0:T(4,128)(2,1)S(1)}, u32[]{:S(2)}, u32[]{:S(2)}) async-start(bf16[4,4,4096]{2,1,0:T(4,128)(2,1)} %reshape.46), calls=%async_computation.2 | async-start | bytes 262144 | tf_op jit(solution)/shard_map/all_to_all | solution.py:56
  91.2 0.6 pad_maximum_fusion
  91.8 5.3 %all-to-all-done.1 = bf16[4,4,4096]{2,1,0:T(4,128)(2,1)S(1)} async-done(((bf16[4,4,4096]{2,1,0:T(4,128)(2,1)}), bf16[4,4,4096]{2,1,0:T(4,128)(2,1)S(1)}, u32[]{:S(2)}, u32[]{:S(2)}) %all-to-all-start.1) | async-done | bytes 131104 | tf_op jit(solution)/shard_map/all_to_all | solution.py:56
  97.1 0.9 fusion.6
  (10 shorter events, 0.1 us)
Async XLA Ops:
  7.2 1.1 %copy-start = (bf16[8,4096]{1,0:T(8,128)(2,1)S(1)}, bf16[8,4096]{1,0:T(8,128)(2,1)}, u32[]{:S(2)}) copy-start(bf16[8,4096]{1,0:T(8,128)(2,1)} %param.6) | copy-start | bytes 196612
  7.2 79.0 %reduce-scatter.2.cloned.1.call-start = ((), (), s32[]{:S(2)}) async-start(), calls=%async_computation.3 | async-start | bytes 1310720 | tf_op jit(solution)/shard_map/reduce_scatter | solution.py:49
  36.7 14.7 %copy-start.2 = (bf16[4096,4]{0,1:T(4,128)(2,1)S(1)}, bf16[4096,4]{0,1:T(4,128)(2,1)}, u32[]{:S(2)}) copy-start(bf16[4096,4]{0,1:T(4,128)(2,1)} %param.7) | copy-start | bytes 98308
  36.7 49.5 %copy-start.1 = (s32[8,2]{0,1:T(2,128)S(1)}, s32[8,2]{0,1:T(2,128)}, u32[]{:S(2)}) copy-start(s32[8,2]{0,1:T(2,128)} %param.11) | copy-start | bytes 196
  87.9 9.2 %all-to-all-start.1 = ((bf16[4,4,4096]{2,1,0:T(4,128)(2,1)}), bf16[4,4,4096]{2,1,0:T(4,128)(2,1)S(1)}, u32[]{:S(2)}, u32[]{:S(2)}) async-start(bf16[4,4,4096]{2,1,0:T(4,128)(2,1)} %reshape.46), calls=%async_computation.2 | async-start | bytes 262144 | tf_op jit(solution)/shard_map/all_to_all | solution.py:56
Sparse Core Ops, SparseCore 0:
  51.4 23.4 reduce-scatter.1
where the time goes:
time: 105 us
  blocking collectives  51.3 us (49%)
  matrix products  24.7 us (24%)
  between operations  15.4 us (15%)
  waiting for transfers between devices  5.32 us (5%)
  other arithmetic  3.94 us (4%)
  starting transfers between devices  3.36 us (3%)
    psum x1, blocking collectives, shards(): lax.psum((square_part, prob_part, count_part), ('expert', 'cuts'))  32 us
    dot_general x1, matrix products, shards(): jnp.dot(flat_hidden, w_down, preferred_element_type=jnp.float32)  14.6 us
    all_to_all x1, blocking collectives, shards(): lax.all_to_all(outbox, 'expert', split_axis=0, concat_axis=0, tiled=True)  12.2 us
    dot_general x1, matrix products, shards(): gate = jnp.dot(flat, w_gate, preferred_element_type=jnp.float32)  8.79 us
    all_gather x1, blocking collectives, shards(): block = lax.all_gather(inbox, 'cuts', axis=0, tiled=True)  7.16 us
    all_to_all x1, waiting for transfers between devices, shards(): lax.all_to_all(answer, 'expert', split_axis=0, concat_axis=0, tiled=True)  5.28 us
    all_to_all x1, starting transfers between devices, shards(): lax.all_to_all(answer, 'expert', split_axis=0, concat_axis=0, tiled=True)  3.32 us
  transfers between devices with their start and end apart: 2, of which 1 were waited for; matrix products, arithmetic and copies ran while one was open for 2% of the time, Pallas kernels for 0%

commit v1 on v0

v1 whole, which is shorter than its diff:
```python
import functools

import jax
import jax.numpy as jnp
from jax import lax
from jax.experimental import pallas as pl
from jax.experimental.pallas import tpu as pltpu
from jax.sharding import PartitionSpec as P

MESH = pl.DeviceIdType.MESH
PACK = 16


def remote(src, dst, send, recv, axis, peer):
    return pltpu.make_async_remote_copy(
        src_ref=src,
        dst_ref=dst,
        send_sem=send,
        recv_sem=recv,
        device_id={axis: peer},
        device_id_type=MESH,
    )


def fold(rows, parts):
    lanes = rows.shape[1] // parts
    return jnp.concatenate([rows[:, q * lanes : (q + 1) * lanes] for q in range(parts)], axis=0)


def kernel(
    dims,
    tokens_ref,
    router_ref,
    ids_ref,
    gate_hbm,
    up_hbm,
    down_hbm,
    mixed_ref,
    stats_ref,
    w_gate,
    w_up,
    w_down,
    outbox,
    inbox,
    block,
    hidden,
    partial,
    sums_in,
    back_out,
    back_in,
    stat_own,
    stat_mid,
    stat_z,
    stat_c,
    weights_sem,
    down_sem,
    a_send,
    a_recv,
    b_send,
    b_recv,
    s_send,
    s_recv,
    t_send,
    t_recv,
    zs_send,
    zs_recv,
    cs_send,
    cs_recv,
):
    E, C, R, cap, D, F, FC, NF, NC, NN = dims
    Q = PACK // cap
    L = D // Q
    LC = NC // Q
    G = E * cap
    me_e = lax.axis_index("expert")
    me_c = lax.axis_index("cuts")

    def ring(me, step, size):
        return lax.rem(me + step, size)

    def gate_copy(i, n):
        cols = pl.ds(pl.multiple_of(n * FC, FC), FC)
        src, dst = ((gate_hbm, w_gate), (up_hbm, w_up))[i]
        return pltpu.make_async_copy(src.at[0, :, cols], dst.at[:, cols], weights_sem.at[i, n])

    def down_copy(n):
        cols = pl.ds(pl.multiple_of(n * NC, NC), NC)
        return pltpu.make_async_copy(down_hbm.at[0, :, cols], w_down.at[:, cols], down_sem.at[n])

    for n in range(NF):
        gate_copy(0, n).start()
        gate_copy(1, n).start()
    for n in range(NN):
        down_copy(n).start()

    barrier = pltpu.get_barrier_semaphore()
    for d in range(1, E):
        pl.semaphore_signal(
            barrier, inc=1, device_id={"expert": ring(me_e, d, E)}, device_id_type=MESH
        )
    for d in range(1, C):
        pl.semaphore_signal(
            barrier, inc=1, device_id={"cuts": ring(me_c, d, C)}, device_id_type=MESH
        )

    ids = ids_ref[...]
    id0, id1 = ids[:, 0:1], ids[:, 1:2]
    row_i = lax.broadcasted_iota(jnp.int32, (R, R), 0)
    col_i = lax.broadcasted_iota(jnp.int32, (R, R), 1)
    id0_row = jnp.sum(jnp.where(row_i == col_i, id0, 0), axis=0, keepdims=True)
    id1_row = jnp.sum(jnp.where(row_i == col_i, id1, 0), axis=0, keepdims=True)
    slot = lax.broadcasted_iota(jnp.int32, (G, R), 0)
    slot_e, slot_j = slot // cap, slot % cap
    named = (id0_row == slot_e) | (id1_row == slot_e)
    before = (row_i < col_i).astype(jnp.float32)
    place = jnp.dot(named.astype(jnp.float32), before, preferred_element_type=jnp.float32)
    chooser = (named & (place == slot_j.astype(jnp.float32))).astype(jnp.bfloat16)
    tokens = tokens_ref[...]
    picked = jnp.dot(chooser, tokens, preferred_element_type=jnp.float32)
    for e in range(E):
        outbox[e] = fold(picked[e * cap : (e + 1) * cap], Q).astype(jnp.bfloat16)
    inbox[me_c, me_e] = outbox[me_e]

    pl.semaphore_wait(barrier, E - 1 + C - 1)

    def to_expert(d):
        peer = ring(me_e, d, E)
        return remote(
            outbox.at[peer], inbox.at[me_c, me_e], a_send.at[d - 1], a_recv.at[d - 1], "expert", peer
        )

    def from_expert(d):
        src = ring(me_e, E - d, E)
        return remote(
            outbox.at[me_e], inbox.at[me_c, src], a_send.at[d - 1], a_recv.at[d - 1], "expert", src
        )

    def to_cut(p, s):
        src = ring(me_e, E - p, E)
        peer = ring(me_c, s, C)
        return remote(
            inbox.at[me_c, src], inbox.at[me_c, src], b_send.at[p, s - 1], b_recv.at[p, s - 1], "cuts", peer
        )

    def from_cut(p, s):
        src = ring(me_e, E - p, E)
        peer = ring(me_c, C - s, C)
        return remote(
            inbox.at[me_c, src], inbox.at[peer, src], b_send.at[p, s - 1], b_recv.at[p, s - 1], "cuts", peer
        )

    for d in range(1, E):
        to_expert(d).start()
    for s in range(1, C):
        to_cut(0, s).start()

    wide = tokens.astype(jnp.float32)
    exps = []
    for e in range(E):
        weight = router_ref[e : e + 1, :].astype(jnp.float32)
        exps.append(jnp.exp(jnp.sum(wide * weight, axis=1, keepdims=True)))
    total = functools.reduce(jnp.add, exps)
    log_total = jnp.log(total)
    probs = [x / total for x in exps]
    member = [((id0 == e) | (id1 == e)).astype(jnp.float32) for e in range(E)]
    chosen = functools.reduce(jnp.add, [m * p for m, p in zip(member, probs)])
    lane = lax.broadcasted_iota(jnp.int32, (R, 128), 1)
    first = jnp.where(lane == E, log_total * log_total, 0.0)
    second = jnp.zeros((R, 128), jnp.float32)
    for e in range(E):
        first = jnp.where(lane == e, probs[e], first)
        second = jnp.where(lane == e, member[e], second)
    stat_own[0] = first
    stat_own[1] = second

    spot = lax.broadcasted_iota(jnp.int32, (R, G), 1)
    spot_e, spot_j = spot // cap, spot % cap
    named_t = ((id0 == spot_e) | (id1 == spot_e))
    after = (col_i < row_i).astype(jnp.float32)
    place_t = jnp.dot(after, named_t.astype(jnp.float32), preferred_element_type=jnp.float32)
    mix = jnp.zeros((R, G), jnp.float32)
    for e in range(E):
        mix = jnp.where(spot_e == e, probs[e] / chosen, mix)
    mix = jnp.where(named_t & (place_t == spot_j.astype(jnp.float32)), mix, 0.0)

    def stat_to_expert(d):
        peer = ring(me_e, d, E)
        return remote(stat_own, stat_z.at[d - 1], zs_send.at[d - 1], zs_recv.at[d - 1], "expert", peer)

    def stat_to_cut(s):
        peer = ring(me_c, s, C)
        return remote(stat_mid, stat_c.at[s - 1], cs_send.at[s - 1], cs_recv.at[s - 1], "cuts", peer)

    for d in range(1, E):
        stat_to_expert(d).start()

    for d in range(1, E):
        from_expert(d).wait_recv()
        for s in range(1, C):
            to_cut(d, s).start()

    def unpack(s):
        owner = ring(me_c, C - s, C)
        arrived = inbox[owner].astype(jnp.float32)
        for q in range(Q):
            rows = jnp.concatenate(
                [arrived[e, q * cap : (q + 1) * cap, :] for e in range(E)], axis=0
            )
            block[pl.ds(pl.multiple_of(owner * G, G), G), q * L : (q + 1) * L] = rows.astype(
                jnp.bfloat16
            )

    unpack(0)
    for d in range(1, E):
        stat_to_expert(d).wait_recv()
    stat = jnp.zeros(stat_own.shape, jnp.float32)
    for e in range(E):
        term = jnp.where(me_e == e, stat_own[...], 0.0)
        for d in range(1, E):
            term = term + jnp.where(ring(me_e, E - d, E) == e, stat_z[d - 1], 0.0)
        stat = stat + term
    stat_mid[...] = stat
    for s in range(1, C):
        stat_to_cut(s).start()

    @pl.loop(1, C)
    def _(s):
        for p in range(E):
            from_cut(p, s).wait_recv()
        unpack(s)

    @pl.loop(0, NF)
    def _(n):
        cols = pl.ds(pl.multiple_of(n * FC, FC), FC)
        gate_copy(0, n).wait()
        gate = jnp.dot(block[...], w_gate[:, cols], preferred_element_type=jnp.float32)
        gate_copy(1, n).wait()
        upper = jnp.dot(block[...], w_up[:, cols], preferred_element_type=jnp.float32)
        hidden[:, cols] = (gate / (1.0 + jnp.exp(-gate)) * upper).astype(jnp.bfloat16)

    def to_sum(n, s):
        peer = ring(me_c, s, C)
        rows = pl.ds(pl.multiple_of(peer * G, G), G)
        return remote(
            partial.at[n, rows], sums_in.at[n, s - 1], s_send.at[n, s - 1], s_recv.at[n, s - 1], "cuts", peer
        )

    def to_owner(n, d):
        peer = ring(me_e, d, E)
        return remote(
            back_out.at[n, peer], back_in.at[n, me_e], t_send.at[n, d - 1], t_recv.at[n, d - 1], "expert", peer
        )

    def from_owner(n, d):
        src = ring(me_e, E - d, E)
        return remote(
            back_out.at[n, me_e], back_in.at[n, src], t_send.at[n, d - 1], t_recv.at[n, d - 1], "expert", src
        )

    def stage_down(n):
        cols = pl.ds(pl.multiple_of(n * NC, NC), NC)
        down_copy(n).wait()
        partial[n] = jnp.dot(
            hidden[...], w_down[:, cols], preferred_element_type=jnp.float32
        ).astype(jnp.bfloat16)
        for s in range(1, C):
            to_sum(n, s).start()

    def stage_sum(n):
        rows = pl.ds(pl.multiple_of(me_c * G, G), G)
        acc = partial[n, rows].astype(jnp.float32)
        for s in range(1, C):
            to_sum(n, s).wait_recv()
            acc = acc + sums_in[n, s - 1].astype(jnp.float32)
        for e in range(E):
            back_out[n, e] = fold(acc[e * cap : (e + 1) * cap], Q).astype(jnp.bfloat16)
        for d in range(1, E):
            to_owner(n, d).start()
        back_in[n, me_e] = back_out[n, me_e]

    def stage_mix(n):
        for d in range(1, E):
            from_owner(n, d).wait_recv()
        got = back_in[n].astype(jnp.float32)
        wide = jnp.concatenate(
            [
                jnp.concatenate([got[e, q * cap : (q + 1) * cap, :] for e in range(E)], axis=0)
                for q in range(Q)
            ],
            axis=1,
        )
        out = jnp.dot(
            mix, wide, preferred_element_type=jnp.float32, precision=lax.Precision.HIGHEST
        )
        mixed_ref[:, n * NC : (n + 1) * NC] = out.astype(jnp.bfloat16)

    for n in range(NN + 2):
        if n < NN:
            stage_down(n)
        if 1 <= n <= NN:
            stage_sum(n - 1)
        if n >= 2:
            stage_mix(n - 2)

    for s in range(1, C):
        stat_to_cut(s).wait_recv()
    stat = jnp.zeros(stat_own.shape, jnp.float32)
    for c in range(C):
        term = jnp.where(me_c == c, stat_mid[...], 0.0)
        for s in range(1, C):
            term = term + jnp.where(ring(me_c, C - s, C) == c, stat_c[s - 1], 0.0)
        stat = stat + term
    rows = float(R * E * C)
    one = jnp.sum(stat[0], axis=0, keepdims=True) / rows
    two = jnp.sum(stat[1], axis=0, keepdims=True) / (rows * 2.0)
    lane = lax.broadcasted_iota(jnp.int32, (1, 128), 1)
    stats_ref[0] = jnp.sum(jnp.where(lane == E, one, 0.0))
    stats_ref[1] = E * jnp.sum(jnp.where(lane < E, one * two, 0.0))

    for d in range(1, E):
        to_expert(d).wait_send()
        stat_to_expert(d).wait_send()
        for n in range(NN):
            to_owner(n, d).wait_send()
    for s in range(1, C):
        stat_to_cut(s).wait_send()
        for p in range(E):
            to_cut(p, s).wait_send()
        for n in range(NN):
            to_sum(n, s).wait_send()


def shards(tokens, router_weight, gate_weight, up_weight, down_weight, expert_ids):
    R, D = tokens.shape
    E = lax.axis_size("expert")
    C = lax.axis_size("cuts")
    F = gate_weight.shape[2]
    cap = R // 2
    Q = PACK // cap
    FC = min(512, F)
    NF = F // FC
    NC = min(1024, D)
    NN = D // NC
    G = E * cap
    rows = C * G
    dims = (E, C, R, cap, D, F, FC, NF, NC, NN)
    bf16, f32 = jnp.bfloat16, jnp.float32
    vmem = pl.BlockSpec(memory_space=pltpu.VMEM)
    hbm = pl.BlockSpec(memory_space=pl.ANY)
    dma = pltpu.SemaphoreType.DMA
    return pl.pallas_call(
        functools.partial(kernel, dims),
        out_shape=(
            jax.ShapeDtypeStruct((R, D), bf16),
            jax.ShapeDtypeStruct((2,), f32),
        ),
        in_specs=[vmem, vmem, vmem, hbm, hbm, hbm],
        out_specs=(vmem, pl.BlockSpec(memory_space=pltpu.SMEM)),
        scratch_shapes=[
            pltpu.VMEM((D, F), bf16),
            pltpu.VMEM((D, F), bf16),
            pltpu.VMEM((F, D), bf16),
            pltpu.VMEM((E, PACK, D // Q), bf16),
            pltpu.VMEM((C, E, PACK, D // Q), bf16),
            pltpu.VMEM((rows, D), bf16),
            pltpu.VMEM((rows, F), bf16),
            pltpu.VMEM((NN, rows, NC), bf16),
            pltpu.VMEM((NN, C - 1, G, NC), bf16),
            pltpu.VMEM((NN, E, PACK, NC // Q), bf16),
            pltpu.VMEM((NN, E, PACK, NC // Q), bf16),
            pltpu.VMEM((2, R, 128), f32),
            pltpu.VMEM((2, R, 128), f32),
            pltpu.VMEM((E - 1, 2, R, 128), f32),
            pltpu.VMEM((C - 1, 2, R, 128), f32),
            dma((2, NF)),
            dma((NN,)),
            dma((E - 1,)),
            dma((E - 1,)),
            dma((E, C - 1)),
            dma((E, C - 1)),
            dma((NN, C - 1)),
            dma((NN, C - 1)),
            dma((NN, E - 1)),
            dma((NN, E - 1)),
            dma((E - 1,)),
            dma((E - 1,)),
            dma((C - 1,)),
            dma((C - 1,)),
        ],
        compiler_params=pltpu.CompilerParams(
            collective_id=0, has_side_effects=True, vmem_limit_bytes=60 * 1024 * 1024
        ),
        cost_estimate=pl.CostEstimate(
            flops=6 * rows * D * F, bytes_accessed=6 * D * F, transcendentals=rows * F
        ),
    )(tokens, router_weight.T, expert_ids, gate_weight, up_weight, down_weight)


def solution(mesh):
    placed = (
        P(("groups", "expert", "cuts"), None),
        P(),
        P("expert", None, "cuts"),
        P("expert", None, "cuts"),
        P("expert", "cuts", None),
        P(("groups", "expert", "cuts"), None),
    )
    return jax.shard_map(
        shards,
        mesh=mesh,
        in_specs=placed,
        out_specs=(P(("groups", "expert", "cuts"), None), P("groups")),
        check_vma=False,
    )
```

time: 105 us -> 43.1 us (0.41)
  blocking collectives: 51.3 us -> 0 us
  Pallas kernels: 0 us -> 38.3 us
  matrix products: 24.7 us -> 0 us
  between operations: 15.4 us -> 0.64 us
  waiting for transfers between devices: 5.32 us -> 0 us
  other arithmetic: 3.94 us -> 0 us
  starting transfers between devices: 3.36 us -> 0 us
  local copies, waits for them, and re-layouts: 0.83 us -> 3.94 us
    pallas_call x0 -> x1, Pallas kernels: none -> 38.3 us  [shards(): pl.pallas_call(functools.partial(kernel, dims), out_shape=(jax.ShapeDtype...]
    psum x1 -> x0, blocking collectives: 32 us -> none  [shards(): lax.psum((square_part, prob_part, count_part), ('expert', 'cuts'))]
    dot_general x5 -> x0, matrix products: 24.7 us -> none  [the longest x1 14.6 us: shards(): jnp.dot(flat_hidden, w_down, preferred_element_type=jnp.float32)]
    all_to_all x1 -> x0, blocking collectives: 12.2 us -> none  [shards(): lax.all_to_all(outbox, 'expert', split_axis=0, concat_axis=0, tiled=True)]
    all_gather x1 -> x0, blocking collectives: 7.16 us -> none  [shards(): block = lax.all_gather(inbox, 'cuts', axis=0, tiled=True)]
    all_to_all x1 -> x0, waiting for transfers between devices: 5.28 us -> none  [shards(): lax.all_to_all(answer, 'expert', split_axis=0, concat_axis=0, tiled=True)]
    unnamed x6 -> x3, local copies, waits for them, and re-layouts: 0.02 us -> 3.94 us
    all_to_all x1 -> x0, starting transfers between devices: 3.32 us -> none  [shards(): lax.all_to_all(answer, 'expert', split_axis=0, concat_axis=0, tiled=True)]
  transfers between devices with their start and end apart: 2 -> 0, of which waited for: 1 -> 0; matrix products, arithmetic and copies ran while one was open for 2% -> 0% of each run, Pallas kernels for 0% -> 0%
where the time goes in v1:
time: 43.1 us; the launch traced here: 42.9 us
  Pallas kernels  38.3 us (89%)
  local copies, waits for them, and re-layouts  3.94 us (9%)
  between operations  0.64 us (1%)
    pallas_call x1, Pallas kernels, shards(): pl.pallas_call(functools.partial(kernel, dims), out_shape=(jax.ShapeDtype...  38.3 us
    unnamed x3, local copies, waits for them, and re-layouts  3.94 us

profile of v1, /device:TPU:0, one launch (start us, length us, event | category | flops | bytes accessed | tf_op | source)
XLA Modules:
  0.0 42.9 jit_solution(14882397068895649623)
XLA Ops:
  0.6 1.3 %copy.8.ids_ref = s32[8,2]{1,0:T(8,128)} copy(s32[8,2]{0,1:T(2,128)} %param.11) | data formatting | bytes 128 | tf_op args[5]
  2.0 38.3 %shard_map.77 = (bf16[8,4096]{1,0:T(8,128)(2,1)}, f32[2]{0:T(128)}) custom-call(bf16[8,4096]{1,0:T(8,128)(2,1)} %tokens_ref.1, bf16[4,4096]{1,0:T(4,128)(2,1)} %bitcast.1, s32[8,2]{1,0:T(8,128)} %copy.8.ids_ref, bf16[1,4096,2048]{2,1,0:T(8,128)(2,1)} %gate_hbm.1, bf16[1,4096,2048]{2,1,0:T(8,128)(2,1)} %up_hbm.1, bf16[1,2048,4096]{2,1,0:T(8,128)(2,1)} %down_hbm.1), custom_call_target="tpu_custom_call" | custom-call | flops 3221225472 | bytes 50331648 | tf_op jit(solution)/shard_map/pallas_call | solution.py:351
  40.3 1.5 %copy.11 = bf16[8,4096]{1,0:T(8,128)(2,1)} copy(bf16[8,4096]{1,0:T(8,128)(2,1)} %get-tuple-element.4) | data formatting | bytes 131072
  41.8 1.1 %copy.12 = f32[2]{0:T(128)} copy(f32[2]{0:T(128)} %get-tuple-element.5) | data formatting | bytes 16

commit v2 on v1

--- a/solution.py
+++ b/solution.py
@@ -9,6 +9,7 @@
 
 MESH = pl.DeviceIdType.MESH
 PACK = 16
+LAG = 4
 
 
 def remote(src, dst, send, recv, axis, peer):
@@ -25,6 +26,12 @@
 def fold(rows, parts):
     lanes = rows.shape[1] // parts
     return jnp.concatenate([rows[:, q * lanes : (q + 1) * lanes] for q in range(parts)], axis=0)
+
+
+def hand_on(rows_ref, stats_ref, rows_out, stats_out):
+    rows_out[...] = rows_ref[...]
+    stats_out[0] = stats_ref[0]
+    stats_out[1] = stats_ref[1]
 
 
 def kernel(
@@ -104,11 +111,11 @@
         )
 
     ids = ids_ref[...]
-    id0, id1 = ids[:, 0:1], ids[:, 1:2]
+    id0_row, id1_row = ids[0:1, :], ids[1:2, :]
     row_i = lax.broadcasted_iota(jnp.int32, (R, R), 0)
     col_i = lax.broadcasted_iota(jnp.int32, (R, R), 1)
-    id0_row = jnp.sum(jnp.where(row_i == col_i, id0, 0), axis=0, keepdims=True)
-    id1_row = jnp.sum(jnp.where(row_i == col_i, id1, 0), axis=0, keepdims=True)
+    id0 = jnp.sum(jnp.where(row_i == col_i, id0_row, 0), axis=1, keepdims=True)
+    id1 = jnp.sum(jnp.where(row_i == col_i, id1_row, 0), axis=1, keepdims=True)
     slot = lax.broadcasted_iota(jnp.int32, (G, R), 0)
     slot_e, slot_j = slot // cap, slot % cap
     named = (id0_row == slot_e) | (id1_row == slot_e)
@@ -153,6 +160,11 @@
         to_expert(d).start()
     for s in range(1, C):
         to_cut(0, s).start()
+
+    for d in range(1, E):
+        from_expert(d).wait_recv()
+        for s in range(1, C):
+            to_cut(d, s).start()
 
     wide = tokens.astype(jnp.float32)
     exps = []
@@ -194,11 +206,6 @@
     for d in range(1, E):
         stat_to_expert(d).start()
 
-    for d in range(1, E):
-        from_expert(d).wait_recv()
-        for s in range(1, C):
-            to_cut(d, s).start()
-
     def unpack(s):
         owner = ring(me_c, C - s, C)
         arrived = inbox[owner].astype(jnp.float32)
@@ -211,6 +218,21 @@
             )
 
     unpack(0)
+    @pl.loop(1, C)
+    def _(s):
+        for p in range(E):
+            from_cut(p, s).wait_recv()
+        unpack(s)
+
+    @pl.loop(0, NF)
+    def _(n):
+        cols = pl.ds(pl.multiple_of(n * FC, FC), FC)
+        gate_copy(0, n).wait()
+        gate = jnp.dot(block[...], w_gate[:, cols], preferred_element_type=jnp.float32)
+        gate_copy(1, n).wait()
+        upper = jnp.dot(block[...], w_up[:, cols], preferred_element_type=jnp.float32)
+        hidden[:, cols] = (gate / (1.0 + jnp.exp(-gate)) * upper).astype(jnp.bfloat16)
+
     for d in range(1, E):
         stat_to_expert(d).wait_recv()
     stat = jnp.zeros(stat_own.shape, jnp.float32)
@@ -222,21 +244,6 @@
     stat_mid[...] = stat
     for s in range(1, C):
         stat_to_cut(s).start()
-
-    @pl.loop(1, C)
-    def _(s):
-        for p in range(E):
-            from_cut(p, s).wait_recv()
-        unpack(s)
-
-    @pl.loop(0, NF)
-    def _(n):
-        cols = pl.ds(pl.multiple_of(n * FC, FC), FC)
-        gate_copy(0, n).wait()
-        gate = jnp.dot(block[...], w_gate[:, cols], preferred_element_type=jnp.float32)
-        gate_copy(1, n).wait()
-        upper = jnp.dot(block[...], w_up[:, cols], preferred_element_type=jnp.float32)
-        hidden[:, cols] = (gate / (1.0 + jnp.exp(-gate)) * upper).astype(jnp.bfloat16)
 
     def to_sum(n, s):
         peer = ring(me_c, s, C)
@@ -294,13 +301,13 @@
         )
         mixed_ref[:, n * NC : (n + 1) * NC] = out.astype(jnp.bfloat16)
 
-    for n in range(NN + 2):
+    for n in range(NN + 2 * LAG):
         if n < NN:
             stage_down(n)
-        if 1 <= n <= NN:
-            stage_sum(n - 1)
-        if n >= 2:
-            stage_mix(n - 2)
+        if LAG <= n < NN + LAG:
+            stage_sum(n - LAG)
+        if n >= 2 * LAG:
+            stage_mix(n - 2 * LAG)
 
     for s in range(1, C):
         stat_to_cut(s).wait_recv()
@@ -348,7 +355,7 @@
     vmem = pl.BlockSpec(memory_space=pltpu.VMEM)
     hbm = pl.BlockSpec(memory_space=pl.ANY)
     dma = pltpu.SemaphoreType.DMA
-    return pl.pallas_call(
+    rows_out, stats = pl.pallas_call(
         functools.partial(kernel, dims),
         out_shape=(
             jax.ShapeDtypeStruct((R, D), bf16),
@@ -393,7 +400,14 @@
         cost_estimate=pl.CostEstimate(
             flops=6 * rows * D * F, bytes_accessed=6 * D * F, transcendentals=rows * F
         ),
-    )(tokens, router_weight.T, expert_ids, gate_weight, up_weight, down_weight)
+    )(tokens, router_weight.T, expert_ids.T, gate_weight, up_weight, down_weight)
+    smem = pl.BlockSpec(memory_space=pltpu.SMEM)
+    return pl.pallas_call(
+        hand_on,
+        out_shape=(jax.ShapeDtypeStruct((R, D), bf16), jax.ShapeDtypeStruct((2,), f32)),
+        in_specs=[vmem, smem],
+        out_specs=(vmem, smem),
+    )(rows_out, stats)
 
 
 def solution(mesh):

time: 43.1 us -> 37.1 us (0.86)
  local copies, waits for them, and re-layouts: 3.94 us -> 0 us
  Pallas kernels: 38.3 us -> 36.2 us
    unnamed x3 -> x0, local copies, waits for them, and re-layouts: 3.94 us -> none
    pallas_call x1, Pallas kernels: 38.3 us -> 34.7 us  [shards(): pl.pallas_call(functools.partial(kernel, dims), out_shape=(jax.ShapeDtype...]
    pallas_call x0 -> x1, Pallas kernels: none -> 1.49 us  [shards(): pl.pallas_call(hand_on, out_shape=(jax.ShapeDtypeStruct((R, D), bf16), ja...]
where the time goes in v2:
time: 37.1 us; the launch traced here: 36.9 us
  Pallas kernels  36.2 us (98%)
  between operations  0.64 us (2%)
    pallas_call x1, Pallas kernels, shards(): pl.pallas_call(functools.partial(kernel, dims), out_shape=(jax.ShapeDtype...  34.7 us
    pallas_call x1, Pallas kernels, shards(): pl.pallas_call(hand_on, out_shape=(jax.ShapeDtypeStruct((R, D), bf16), ja...  1.49 us

profile of v2, /device:TPU:0, one launch (start us, length us, event | category | flops | bytes accessed | tf_op | source)
XLA Modules:
  0.0 36.9 jit_solution(10096102170454209434)
XLA Ops:
  0.6 34.7 %shard_map.77 = (bf16[8,4096]{1,0:T(8,128)(2,1)}, f32[2]{0:T(128)}) custom-call(bf16[8,4096]{1,0:T(8,128)(2,1)} %tokens_ref.1, bf16[4,4096]{1,0:T(4,128)(2,1)} %bitcast.2, s32[2,8]{1,0:T(2,128)} %bitcast.3, bf16[1,4096,2048]{2,1,0:T(8,128)(2,1)} %gate_hbm.1, bf16[1,4096,2048]{2,1,0:T(8,128)(2,1)} %up_hbm.1, bf16[1,2048,4096]{2,1,0:T(8,128)(2,1)} %down_hbm.1), custom_call_target="tpu_custom_call" | custom-call | flops 3221225472 | bytes 50331648 | tf_op jit(solution)/shard_map/pallas_call | solution.py:358
  35.4 1.5 %shard_map.78 = (bf16[8,4096]{1,0:T(8,128)(2,1)}, f32[2]{0:T(128)}) custom-call(bf16[8,4096]{1,0:T(8,128)(2,1)} %get-tuple-element.4.rows_ref, f32[2]{0:T(128)} %get-tuple-element.5.stats_ref), custom_call_target="tpu_custom_call" | custom-call | tf_op jit(solution)/shard_map/pallas_call | solution.py:405

commit v3 on v2

--- a/solution.py
+++ b/solution.py
@@ -344,7 +344,7 @@
     F = gate_weight.shape[2]
     cap = R // 2
     Q = PACK // cap
-    FC = min(512, F)
+    FC = min(1024, F)
     NF = F // FC
     NC = min(1024, D)
     NN = D // NC

time: 37.1 us -> 36.5 us (0.984)
  Pallas kernels: 36.2 us -> 35.7 us
    pallas_call x1, Pallas kernels: 34.7 us -> 34.2 us  [shards(): pl.pallas_call(functools.partial(kernel, dims), out_shape=(jax.ShapeDtype...]
where the time goes in v3:
time: 36.5 us; the launch traced here: 36.3 us
  Pallas kernels  35.7 us (98%)
  between operations  0.64 us (2%)
    pallas_call x1, Pallas kernels, shards(): pl.pallas_call(functools.partial(kernel, dims), out_shape=(jax.ShapeDtype...  34.2 us
    pallas_call x1, Pallas kernels, shards(): pl.pallas_call(hand_on, out_shape=(jax.ShapeDtypeStruct((R, D), bf16), ja...  1.49 us

profile of v3, /device:TPU:0, one launch (start us, length us, event | category | flops | bytes accessed | tf_op | source)
XLA Modules:
  0.0 36.3 jit_solution(382989005158330614)
XLA Ops:
  0.6 34.2 %shard_map.77 = (bf16[8,4096]{1,0:T(8,128)(2,1)}, f32[2]{0:T(128)}) custom-call(bf16[8,4096]{1,0:T(8,128)(2,1)} %tokens_ref.1, bf16[4,4096]{1,0:T(4,128)(2,1)} %bitcast.2, s32[2,8]{1,0:T(2,128)} %bitcast.3, bf16[1,4096,2048]{2,1,0:T(8,128)(2,1)} %gate_hbm.1, bf16[1,4096,2048]{2,1,0:T(8,128)(2,1)} %up_hbm.1, bf16[1,2048,4096]{2,1,0:T(8,128)(2,1)} %down_hbm.1), custom_call_target="tpu_custom_call" | custom-call | flops 3221225472 | bytes 50331648 | tf_op jit(solution)/shard_map/pallas_call | solution.py:358
  34.8 1.5 %shard_map.78 = (bf16[8,4096]{1,0:T(8,128)(2,1)}, f32[2]{0:T(128)}) custom-call(bf16[8,4096]{1,0:T(8,128)(2,1)} %get-tuple-element.4.rows_ref, f32[2]{0:T(128)} %get-tuple-element.5.stats_ref), custom_call_target="tpu_custom_call" | custom-call | tf_op jit(solution)/shard_map/pallas_call | solution.py:405
